TPU v7x, 32 devices: a whole 2x2x4 slice. The times are simulated.
32 devices in a mesh: layer: 2 (over y), latent: 16 (over z, x, core).
Axes of the slice: x: 2, y: 2, z: 4, core: 2. Of those that a mesh axis runs over, the one named last changes fastest.
Arguments:
- acts: bfloat16 [1280, 4608], P(None, 'layer'), may hold values from -6 to 6
- enc_weight: bfloat16 [4608, 32768], P('layer', 'latent'), may hold values from -0.09375 to 0.09375
- enc_bias: float32 [32768], P('latent'), may hold values from -3 to 3
- dec_weight: bfloat16 [32768, 4608], P('latent', 'layer'), may hold values from -0.3314563 to 0.3314563, as said below
- dec_bias: float32 [4608], P('layer'), may hold values from -2 to 2
Outputs:
- grad_enc: float32 [4608, 32768], P('layer', 'latent')
- grad_enc_bias: float32 [32768], P('latent')
- grad_dec: float32 [32768, 4608], P('latent', 'layer')
- grad_dec_bias: float32 [4608], P('layer')
Inputs may be any that keep to these rules, and one draw needn't show every extreme that they name: `dec_weight`: decoder entries lie within 60 / sqrt(32768) of zero.
All inputs are finite; a program needn't handle non-finite values.
Results may differ from a plain program's by a relative error of at most 0.0045.
Values may be sent and summed in bfloat16 or wider, within the bound.
A program may use at most 192 MiB of HBM per device.

v0:
```python
import jax
import jax.numpy as jnp
from jax import lax
from jax.sharding import PartitionSpec as P


def per_device(acts, enc_weight, enc_bias, dec_weight, dec_bias):
    rows_all = acts.shape[0]
    scale = 1.0 / jnp.sqrt(jnp.float32(rows_all))
    sparsity = 1.0
    dec_f = dec_weight.astype(jnp.float32)
    squares = jnp.sum(dec_f * dec_f, axis=1)
    partial_pre = jnp.dot(acts, enc_weight, preferred_element_type=jnp.float32)
    summed_pre, summed_sq = lax.psum((partial_pre, squares), "layer")
    pre = summed_pre + enc_bias
    codes = jax.nn.softplus(pre).astype(jnp.bfloat16)
    slope = jax.nn.sigmoid(pre)
    norms = jnp.sqrt(summed_sq + 1e-06)
    partial_recon = jnp.dot(codes, dec_weight, preferred_element_type=jnp.float32)
    recon = lax.psum(partial_recon, "latent") + dec_bias
    err_grad = (2.0 * scale * (recon - acts.astype(jnp.float32))).astype(jnp.bfloat16)
    grad_dec_bias = jnp.sum(err_grad.astype(jnp.float32), axis=0)
    column = jnp.sum(codes.astype(jnp.float32), axis=0)
    grad_dec = lax.dot_general(
        codes, err_grad, (((0,), (0,)), ((), ())), preferred_element_type=jnp.float32
    )
    grad_dec = grad_dec + (sparsity * scale * column / norms)[:, None] * dec_f
    partial_back = lax.dot_general(
        err_grad, dec_weight, (((1,), (1,)), ((), ())), preferred_element_type=jnp.float32
    )
    back = lax.psum(partial_back, "layer") + sparsity * scale * norms
    delta = (back * slope).astype(jnp.bfloat16)
    grad_enc = lax.dot_general(
        acts, delta, (((0,), (0,)), ((), ())), preferred_element_type=jnp.float32
    )
    grad_enc_bias = jnp.sum(delta.astype(jnp.float32), axis=0)
    return (grad_enc, grad_enc_bias, grad_dec, grad_dec_bias)


def solution(mesh):
    return jax.shard_map(
        per_device,
        mesh=mesh,
        in_specs=(
            P(None, "layer"),
            P("layer", "latent"),
            P("latent"),
            P("latent", "layer"),
            P("layer"),
        ),
        out_specs=(P("layer", "latent"), P("latent"), P("latent", "layer"), P("layer")),
        check_vma=False,
    )
```

profile of v0, /device:TPU:0, one launch (start us, length us, event | category | flops | bytes accessed | tf_op | source)
XLA Modules:
  0.0 848.5 jit_solution(3419240343869286891)
XLA Ops:
  7.2 0.0 all-reduce.4.cloned.1.call-start
  7.2 19.1 %fusion.5 = f32[1280,2048]{1,0:T(8,128)} fusion(bf16[1280,2304]{1,0:T(8,128)(2,1)} %param.5, bf16[2304,2048]{1,0:T(8,128)(2,1)} %param.6), kind=kOutput, calls=%fused_computation.15 | convolution fusion | flops 12079595520 | bytes 25821184 | tf_op jit(solution)/shard_map/dot_general | solution.py:13
  26.3 0.0 all-reduce.4.cloned.1.call-update
  26.3 0.0 all-reduce.6.cloned.1.call-start
  26.3 246.0 %all-reduce.4.cloned.1.call-done = f32[1280,2048]{1,0:T(8,128)} async-done(((f32[1280,2048]{1,0:T(8,128)}), f32[1280,2048]{1,0:T(8,128)}) %all-reduce.4.cloned.1.call-update) | async-done | bytes 10485776 | tf_op jit(solution)/shard_map/psum | solution.py:14
  272.4 0.0 copy-done.1
  272.4 8.4 convert_reduce_fusion.1
  280.8 0.0 copy-start
  280.8 2.3 copy-done
  283.1 16.7 %fusion.6 = f32[1280,2304]{1,0:T(8,128)} fusion(bf16[1280,2048]{1,0:T(8,128)(2,1)S(1)} %get-tuple-element.11, bf16[2048,2304]{1,0:T(8,128)(2,1)} %param.8), kind=kOutput, calls=%fused_computation.16 | convolution fusion | flops 12079595520 | bytes 26476544 | tf_op jit(solution)/shard_map/dot_general | solution.py:19
  299.7 0.0 all-reduce.6.cloned.1.call-update
  299.8 0.2 all-reduce.8.cloned.1.call-start
  300.0 221.4 %all-reduce.6.cloned.1.call-done = f32[1280,2304]{1,0:T(8,128)} async-done(((f32[1280,2304]{1,0:T(8,128)}), f32[1280,2304]{1,0:T(8,128)}) %all-reduce.6.cloned.1.call-update) | async-done | bytes 11796496 | tf_op jit(solution)/shard_map/psum | solution.py:20
  521.4 0.0 copy-done.2
  521.4 12.3 %convert_reduce_fusion = (f32[2304]{0:T(1024)}, bf16[1280,2304]{1,0:T(8,128)(2,1)}) fusion(bf16[1280,2304]{1,0:T(8,128)(2,1)} %param.5, f32[1280,2304]{1,0:T(8,128)} %all-reduce.6.cloned.1.call-done, f32[2304]{0:T(1024)S(1)} %copy-done.2), kind=kLoop, calls=%fused_computation.6 | loop fusion | flops 20641536 | bytes 23611392 | tf_op jit(solution)/shard_map/reduce_sum | solution.py:22
  533.7 19.1 %fusion.7 = f32[1280,2048]{1,0:T(8,128)} fusion(bf16[1280,2304]{1,0:T(8,128)(2,1)} %get-tuple-element.9, bf16[2048,2304]{1,0:T(8,128)(2,1)} %param.8), kind=kOutput, calls=%fused_computation.17 | convolution fusion | flops 12079595520 | bytes 25821184 | tf_op jit(solution)/shard_map/dot_general | solution.py:28
  552.8 0.0 all-reduce.8.cloned.1.call-update
  552.9 5.6 fusion
  558.4 5.2 psum.31
  563.6 21.6 %fusion.1 = f32[2048,2304]{1,0:T(8,128)} fusion(bf16[2048,2304]{1,0:T(8,128)(2,1)} %param.8, bf16[1280,2048]{1,0:T(8,128)(2,1)} %copy-done, bf16[1280,2304]{1,0:T(8,128)(2,1)} %get-tuple-element.9, f32[2048]{0:T(1024)S(1)} %get-tuple-element.14), kind=kOutput, calls=%fused_computation.4 | convolution fusion | flops 12093751296 | bytes 39460864 | tf_op jit(solution)/shard_map/dot_general | solution.py:24
  585.2 211.3 %all-reduce.8.cloned.1.call-done = f32[1280,2048]{1,0:T(8,128)} async-done(((f32[1280,2048]{1,0:T(8,128)}), f32[1280,2048]{1,0:T(8,128)}) %all-reduce.8.cloned.1.call-update) | async-done | bytes 10485776 | tf_op jit(solution)/shard_map/psum | solution.py:31
  796.5 8.9 %convert_reduce_fusion.2 = (f32[2048]{0:T(1024)}, bf16[1280,2048]{1,0:T(8,128)(2,1)S(1)}) fusion(f32[1280,2048]{1,0:T(8,128)} %all-reduce.4.cloned.1.call-done, f32[2048]{0:T(1024)S(1)} %copy-done.1, f32[1280,2048]{1,0:T(8,128)} %all-reduce.8.cloned.1.call-done, f32[2048]{0:T(1024)S(1)} %get-tuple-element.15), kind=kLoop, calls=%fused_computation.10 | loop fusion | flops 23590912 | bytes 26238976 | tf_op jit(solution)/shard_map/reduce_sum | solution.py:36
  805.5 17.9 %convolution_bitcast_fusion = f32[2304,2048]{0,1:T(8,128)} fusion(bf16[1280,2048]{1,0:T(8,128)(2,1)S(1)} %get-tuple-element.13, bf16[1280,2304]{1,0:T(8,128)(2,1)} %param.5), kind=kOutput, calls=%fused_computation.5 | convolution fusion | flops 12079595520 | bytes 30015488 | tf_op jit(solution)/shard_map/dot_general | solution.py:33
  823.3 18.6 %copy.9 = f32[2304,2048]{1,0:T(8,128)} copy(f32[2304,2048]{0,1:T(8,128)} %convolution_bitcast_fusion) | data formatting | bytes 37748736
  (3 shorter events, 0.0 us)
Async XLA Ops:
  7.2 265.2 %all-reduce.4.cloned.1.call-start = ((), (), s32[]{:S(2)}) async-start(), calls=%async_computation | async-start | bytes 20971520 | tf_op jit(solution)/shard_map/psum | solution.py:14
  26.3 246.1 %copy-start.1 = (f32[2048]{0:T(1024)S(1)}, f32[2048]{0:T(1024)}, u32[]{:S(2)}) copy-start(f32[2048]{0:T(1024)} %param.7) | copy-start | bytes 24580
  26.3 495.1 %all-reduce.6.cloned.1.call-start = ((), (), s32[]{:S(2)}) async-start(), calls=%async_computation.1 | async-start | bytes 23592960 | tf_op jit(solution)/shard_map/psum | solution.py:20
  280.8 2.3 copy-start
  299.7 221.6 %copy-start.2 = (f32[2304]{0:T(1024)S(1)}, f32[2304]{0:T(1024)}, u32[]{:S(2)}) copy-start(f32[2304]{0:T(1024)} %param.9) | copy-start | bytes 27652
  299.8 496.7 %all-reduce.8.cloned.1.call-start = ((), (), s32[]{:S(2)}) async-start(), calls=%async_computation.2 | async-start | bytes 20971520 | tf_op jit(solution)/shard_map/psum | solution.py:31
Sparse Core Ops, SparseCore 0:
  26.4 245.8 all-reduce.3
  299.9 221.4 all-reduce.5
  553.0 243.4 all-reduce.7
where the time goes:
time: 849 us
  waiting for transfers between devices  679 us (80%)
  matrix products  94.3 us (11%)
  other arithmetic  35.3 us (4%)
  local copies, waits for them, and re-layouts  20.9 us (2%)
  between operations  13.8 us (2%)
    psum x1, waiting for transfers between devices, per_device(): summed_pre, summed_sq = lax.psum((partial_pre, squares), 'layer')  246 us
    psum x1, waiting for transfers between devices, per_device(): recon = lax.psum(partial_recon, 'latent') + dec_bias  221 us
    psum x1, waiting for transfers between devices, per_device(): back = lax.psum(partial_back, 'layer') + sparsity * scale * norms  211 us
    dot_general x1, matrix products, per_device(): lax.dot_general(codes, err_grad, (((0,), (0,)), ((), ())), preferred_elem...  21.6 us
    unnamed x7, local copies, waits for them, and re-layouts  20.9 us
    dot_general x1, matrix products, per_device(): lax.dot_general(err_grad, dec_weight, (((1,), (1,)), ((), ())), preferred...  19.1 us
    dot_general x1, matrix products, per_device(): partial_pre = jnp.dot(acts, enc_weight, preferred_element_type=jnp.float32)  19.1 us
    dot_general x1, matrix products, per_device(): lax.dot_general(acts, delta, (((0,), (0,)), ((), ())), preferred_element_...  17.9 us
  transfers between devices with their start and end apart: 3, of which 3 were waited for; matrix products, arithmetic and copies ran while one was open for 3% of the time, Pallas kernels for 0%

commit v1 on v0

v1 whole, which is shorter than its diff:
```python
import jax
import jax.numpy as jnp
from jax import lax
from jax.sharding import PartitionSpec as P

LOCAL = 4


def split_rows(rows):
    for parts in (5, 4, 2):
        if rows % (parts * 16) == 0:
            return parts
    return 1


def rows_of(array, start, count):
    return lax.dynamic_slice_in_dim(array, start, count, axis=0)


def make_per_device(n_layer, n_latent):
    depth = n_latent // LOCAL

    def swap(array, bit):
        return lax.ppermute(array, "latent", [(i, i ^ bit) for i in range(n_latent)])

    def shift(array, step):
        pairs = [(i, (i + step * LOCAL) % n_latent) for i in range(n_latent)]
        return lax.ppermute(array, "latent", pairs)

    def other_layer(array):
        return lax.ppermute(array, "layer", [(0, 1), (1, 0)])

    def over_layer(array, other):
        own = array.astype(jnp.float32)
        if n_layer == 2:
            return own + other.astype(jnp.float32)
        return lax.psum(own, "layer")

    groups = [[z * LOCAL + c for z in range(depth)] for c in range(LOCAL)]

    def per_device(acts, enc_weight, enc_bias, dec_weight, dec_bias):
        rows = acts.shape[0]
        parts = split_rows(rows)
        part = rows // parts
        scale = 1.0 / jnp.sqrt(jnp.float32(rows))
        sparsity = 1.0
        index = lax.axis_index("latent")
        z, x, core = index // LOCAL, (index // 2) % 2, index % 2

        done = []

        def send_layer(array):
            if n_layer != 2:
                return array, None
            if len(done) >= 2:
                array, earlier = lax.optimization_barrier((array, done[-2]))
                del earlier
            other = other_layer(array)
            done.append(other)
            return array, other

        dec_f = dec_weight.astype(jnp.float32)
        squares = jnp.sum(dec_f * dec_f, axis=1)
        squares = over_layer(squares, other_layer(squares) if n_layer == 2 else None)
        norms = jnp.sqrt(squares + 1e-06)

        def encode(k):
            block = acts[k * part : (k + 1) * part]
            own = jnp.dot(block, enc_weight, preferred_element_type=jnp.float32)
            return send_layer(own.astype(jnp.float16))

        def reduce_latent(partial):
            half, quarter = part // 2, part // 4
            piece = quarter // depth
            got = swap(rows_of(partial, (1 - core) * half, half), 1)
            held = rows_of(partial, core * half, half) + got
            got = swap(rows_of(held, (1 - x) * quarter, quarter).astype(jnp.bfloat16), 2)
            held = rows_of(held, x * quarter, quarter) + got.astype(jnp.float32)
            if depth > 4:
                return lax.psum_scatter(
                    held, "latent", scatter_dimension=0, axis_index_groups=groups, tiled=True
                )
            total = rows_of(held, z * piece, piece)
            for step in range(1, depth):
                target = (z + step) % depth
                got = shift(rows_of(held, target * piece, piece).astype(jnp.bfloat16), step)
                total = total + got.astype(jnp.float32)
            return total

        def gather_latent(own):
            piece = own.shape[0]
            if depth > 4:
                held = lax.all_gather(own, "latent", axis_index_groups=groups, tiled=True)
            else:
                held = jnp.zeros((piece * depth, own.shape[1]), own.dtype)
                held = lax.dynamic_update_slice_in_dim(held, own, z * piece, axis=0)
                for step in range(1, depth):
                    source = (z - step + depth) % depth
                    held = lax.dynamic_update_slice_in_dim(
                        held, shift(own, step), source * piece, axis=0
                    )
            for bit, place in ((2, x), (1, core)):
                got = swap(held, bit)
                low = jnp.where(place == 0, held, got)
                high = jnp.where(place == 0, got, held)
                held = jnp.concatenate([low, high], axis=0)
            return held

        def decode(k, own, other):
            pre = over_layer(own, other) + enc_bias
            codes = jax.nn.softplus(pre).astype(jnp.bfloat16)
            partial = jnp.dot(codes, dec_weight, preferred_element_type=jnp.float32)
            total = reduce_latent(partial)
            piece = total.shape[0]
            start = k * part + core * (part // 2) + x * (part // 4) + z * piece
            mine = rows_of(acts, start, piece).astype(jnp.float32)
            err = (2.0 * scale * (total + dec_bias - mine)).astype(jnp.bfloat16)
            return codes, gather_latent(err)

        def back_of(err):
            own = lax.dot_general(
                err, dec_weight, (((1,), (1,)), ((), ())), preferred_element_type=jnp.float32
            )
            return send_layer(own.astype(jnp.bfloat16))

        pres = [encode(k) for k in range(parts)]
        codes, errs = [], []
        for k in range(parts):
            c, e = decode(k, *pres[k])
            codes.append(c)
            errs.append(e)
        backs = [back_of(e) for e in errs]

        codes = jnp.concatenate(codes, axis=0)
        err_grad = jnp.concatenate(errs, axis=0)
        grad_dec_bias = jnp.sum(err_grad.astype(jnp.float32), axis=0)
        column = jnp.sum(codes.astype(jnp.float32), axis=0)
        grad_dec = lax.dot_general(
            codes, err_grad, (((0,), (0,)), ((), ())), preferred_element_type=jnp.float32
        )
        grad_dec = grad_dec + (sparsity * scale * column / norms)[:, None] * dec_f

        deltas = []
        for k in range(parts):
            slope = jax.nn.sigmoid(over_layer(*pres[k]) + enc_bias)
            back = over_layer(*backs[k]) + sparsity * scale * norms
            deltas.append((back * slope).astype(jnp.bfloat16))
        delta = jnp.concatenate(deltas, axis=0)
        grad_enc = lax.dot_general(
            acts, delta, (((0,), (0,)), ((), ())), preferred_element_type=jnp.float32
        )
        grad_enc_bias = jnp.sum(delta.astype(jnp.float32), axis=0)
        return (grad_enc, grad_enc_bias, grad_dec, grad_dec_bias)

    return per_device


def solution(mesh):
    return jax.shard_map(
        make_per_device(mesh.shape["layer"], mesh.shape["latent"]),
        mesh=mesh,
        in_specs=(
            P(None, "layer"),
            P("layer", "latent"),
            P("latent"),
            P("latent", "layer"),
            P("layer"),
        ),
        out_specs=(P("layer", "latent"), P("latent"), P("latent", "layer"), P("layer")),
        check_vma=False,
    )
```

time: 849 us -> 402 us (0.47)
  waiting for transfers between devices: 679 us -> 137 us
  starting transfers between devices: 0.3 us -> 59.4 us
  matrix products: 94.3 us -> 126 us
  other arithmetic: 35.3 us -> 50.4 us
  between operations: 13.8 us -> 1.81 us
    psum x3 -> x0, waiting for transfers between devices: 679 us -> none  [the longest x1 246 us: per_device(): summed_pre, summed_sq = lax.psum((partial_pre, squares), 'layer')]
    ppermute x0 -> x61, waiting for transfers between devices: none -> 137 us  [the longest x11 65.2 us: other_layer(): return lax.ppermute(array, 'layer', [(0, 1), (1, 0)])]
    ppermute x0 -> x61, starting transfers between devices: none -> 59.4 us  [the longest x30 30.9 us: shift(): return lax.ppermute(array, 'latent', pairs)]
    dot_general x3 -> x15, matrix products: 54.8 us -> 86 us  [the longest x5 38.1 us: decode(): partial = jnp.dot(codes, dec_weight, preferred_element_type=jnp.float32)]
    unnamed x0 -> x17, other arithmetic: none -> 24.6 us
    reduce_sum x1, other arithmetic: 12.3 us -> 1.48 us  [per_device(): grad_dec_bias = jnp.sum(err_grad.astype(jnp.float32), axis=0)]
    reduce_sum x1 -> x0, other arithmetic: 8.94 us -> none  [per_device(): grad_enc_bias = jnp.sum(delta.astype(jnp.float32), axis=0)]
    unnamed x7 -> x55, local copies, waits for them, and re-layouts: 20.9 us -> 19.8 us
  transfers between devices with their start and end apart: 3 -> 61, of which waited for: 3 -> 34; matrix products, arithmetic and copies ran while one was open for 3% -> 30% of each run, Pallas kernels for 0% -> 0%
where the time goes in v1:
time: 402 us; the launch traced here: 398 us
  waiting for transfers between devices  137 us (34%)
  matrix products  126 us (31%)
  starting transfers between devices  59.4 us (15%)
  other arithmetic  50.4 us (13%)
  local copies, waits for them, and re-layouts  22.4 us (6%)
    ppermute x11, waiting for transfers between devices, other_layer(): return lax.ppermute(array, 'layer', [(0, 1), (1, 0)])  65.2 us
    ppermute x30, waiting for transfers between devices, shift(): return lax.ppermute(array, 'latent', pairs)  45.8 us
    dot_general x5, matrix products, decode(): partial = jnp.dot(codes, dec_weight, preferred_element_type=jnp.float32)  38.1 us
    ppermute x30, starting transfers between devices, shift(): return lax.ppermute(array, 'latent', pairs)  30.9 us
    dot_general x5, matrix products, encode(): own = jnp.dot(block, enc_weight, preferred_element_type=jnp.float32)  27.5 us
    ppermute x20, waiting for transfers between devices, swap(): lax.ppermute(array, 'latent', [(i, i ^ bit) for i in range(n_latent)])  26.5 us
    unnamed x17, other arithmetic  24.6 us
    dot_general x1, matrix products, per_device(): lax.dot_general(codes, err_grad, (((0,), (0,)), ((), ())), preferred_elem...  21.8 us
  transfers between devices with their start and end apart: 61, of which 34 were waited for; matrix products, arithmetic and copies ran while one was open for 30% of the time, Pallas kernels for 0%

profile of v1, /device:TPU:0, one launch (start us, length us, event | category | flops | bytes accessed | tf_op | source)
XLA Modules:
  0.0 397.9 jit_solution(9842902155215458191)
XLA Ops:
  0.6 7.8 %convolution_convert_fusion.9 = f16[256,2048]{1,0:T(8,128)(2,1)} fusion(bf16[2304,2048]{1,0:T(8,128)(2,1)} %param.6, bf16[1280,2304]{1,0:T(8,128)(2,1)} %param.5), kind=kOutput, calls=%fused_computation.22 | convolution fusion | flops 2416443392 | bytes 11665408 | tf_op jit(solution)/shard_map/dot_general | solution.py:69
  13.4 7.8 %convolution_convert_fusion.6 = f16[256,2048]{1,0:T(8,128)(2,1)} fusion(bf16[2304,2048]{1,0:T(8,128)(2,1)} %param.6, bf16[1280,2304]{1,0:T(8,128)(2,1)} %param.5), kind=kOutput, calls=%fused_computation.19 | convolution fusion | flops 2416443392 | bytes 11665408 | tf_op jit(solution)/shard_map/dot_general | solution.py:69
  23.2 6.3 %convolution_convert_fusion.7 = f16[256,2048]{1,0:T(8,128)(2,1)S(1)} fusion(bf16[2304,2048]{1,0:T(8,128)(2,1)} %param.6, bf16[1280,2304]{1,0:T(8,128)(2,1)S(1)} %bitcast.24), kind=kOutput, calls=%fused_computation.20 | convolution fusion | flops 2416443392 | bytes 11665408 | tf_op jit(solution)/shard_map/dot_general | solution.py:69
  35.8 8.0 %fusion.45 = f32[256,2304]{1,0:T(8,128)S(1)} fusion(bf16[2048,2304]{1,0:T(8,128)(2,1)} %param.8, f16[256,2048]{1,0:T(8,128)(2,1)} %collective-permute-done, f16[256,2048]{1,0:T(8,128)(2,1)} %convolution_convert_fusion.9, f32[2048]{0:T(1024)S(1)} %copy-done.16), kind=kOutput, calls=%fused_computation.175 | convolution fusion | flops 2421686272 | bytes 13901824 | tf_op jit(solution)/shard_map/dot_general | solution.py:112
  44.0 13.5 %collective-permute-done.11 = f16[256,2048]{1,0:T(8,128)(2,1)} collective-permute-done((f16[256,2048]{1,0:T(8,128)(2,1)}, f16[256,2048]{1,0:T(8,128)(2,1)}, u32[]{:S(2)}, u32[]{:S(2)}) %collective-permute-start.11) | collective-permute-done | bytes 1048608 | tf_op jit(solution)/shard_map/ppermute | solution.py:31
  59.5 8.0 %fusion.43 = f32[256,2304]{1,0:T(8,128)S(1)} fusion(bf16[2048,2304]{1,0:T(8,128)(2,1)} %param.8, f16[256,2048]{1,0:T(8,128)(2,1)} %collective-permute-done.11, f16[256,2048]{1,0:T(8,128)(2,1)} %convolution_convert_fusion.6, f32[2048]{0:T(1024)S(1)} %copy-done.16), kind=kOutput, calls=%fused_computation.174 | convolution fusion | flops 2421686272 | bytes 13901824 | tf_op jit(solution)/shard_map/dot_general | solution.py:112
  67.7 36.6 %collective-permute-done.25 = f16[256,2048]{1,0:T(8,128)(2,1)S(1)} collective-permute-done((f16[256,2048]{1,0:T(8,128)(2,1)S(1)}, f16[256,2048]{1,0:T(8,128)(2,1)S(1)}, u32[]{:S(2)}, u32[]{:S(2)}) %collective-permute-start.25) | collective-permute-done | bytes 1048608 | tf_op jit(solution)/shard_map/ppermute | solution.py:31
  110.7 14.5 %fusion.39 = f32[256,2304]{1,0:T(8,128)S(1)} fusion(bf16[2048,2304]{1,0:T(8,128)(2,1)S(1)} %bitcast.22, f16[256,2048]{1,0:T(8,128)(2,1)S(1)} %collective-permute-done.12, f16[256,2048]{1,0:T(8,128)(2,1)S(1)} %convolution_convert_fusion.7, f32[2048]{0:T(1024)S(1)} %copy-done.16), kind=kOutput, calls=%fused_computation.172 | convolution fusion | flops 2421686272 | bytes 13901824 | tf_op jit(solution)/shard_map/dot_general | solution.py:112
  127.9 7.5 %collective-permute-done.2 = bf16[64,2304]{1,0:T(8,128)(2,1)S(1)} collective-permute-done((bf16[64,2304]{1,0:T(8,128)(2,1)S(1)}, bf16[64,2304]{1,0:T(8,128)(2,1)S(1)}, u32[]{:S(2)}, u32[]{:S(2)}) %collective-permute-start.2) | collective-permute-done | bytes 294944 | tf_op jit(solution)/shard_map/ppermute | solution.py:24
  155.8 3.8 collective-permute-done.6
  191.8 4.8 %convolution_convert_fusion.8 = bf16[256,2048]{1,0:T(8,128)(2,1)} fusion(bf16[2048,2304]{1,0:T(8,128)(2,1)S(1)} %bitcast.22, bf16[128,2304]{1,0:T(8,128)(2,1)} %get-tuple-element.41, bf16[128,2304]{1,0:T(8,128)(2,1)} %get-tuple-element.43), kind=kOutput, calls=%fused_computation.21 | convolution fusion | flops 2418802688 | bytes 11665408 | tf_op jit(solution)/shard_map/dot_general | solution.py:121
  199.1 4.9 %convolution_convert_fusion.5 = bf16[256,2048]{1,0:T(8,128)(2,1)} fusion(bf16[2048,2304]{1,0:T(8,128)(2,1)S(1)} %bitcast.22, bf16[128,2304]{1,0:T(8,128)(2,1)} %get-tuple-element.37, bf16[128,2304]{1,0:T(8,128)(2,1)} %get-tuple-element.39), kind=kOutput, calls=%fused_computation.18 | convolution fusion | flops 2418802688 | bytes 11665408 | tf_op jit(solution)/shard_map/dot_general | solution.py:121
  210.2 4.3 %collective-permute-start.43 = (bf16[16,2304]{1,0:T(8,128)(2,1)S(1)}, bf16[16,2304]{1,0:T(8,128)(2,1)S(1)}, u32[]{:S(2)}, u32[]{:S(2)}) collective-permute-start(bf16[16,2304]{1,0:T(8,128)(2,1)S(1)} %get-tuple-element.72), channel_id=1, source_target_pairs={{0,12},{1,13},{2,14},{3,15},{4,0},{5,1},{6,2},{7,3},{8,4},{9,5},{1... | collective-permute-start | bytes 221192 | tf_op jit(solution)/shard_map/ppermute | solution.py:28
  265.9 4.2 %collective-permute-done.53 = bf16[16,2304]{1,0:T(8,128)(2,1)S(1)} collective-permute-done((bf16[16,2304]{1,0:T(8,128)(2,1)S(1)}, bf16[16,2304]{1,0:T(8,128)(2,1)S(1)}, u32[]{:S(2)}, u32[]{:S(2)}) %collective-permute-start.53) | collective-permute-done | bytes 73760 | tf_op jit(solution)/shard_map/ppermute | solution.py:28
  271.3 3.8 convolution_convert_fusion.1
  284.9 5.3 %constant_dynamic-update-slice_fusion.4 = (bf16[1280,2048]{1,0:T(8,128)(2,1)}, bf16[1280,2048]{1,0:T(8,128)(2,1)}) fusion(f32[2048]{0:T(1024)S(1)} %copy-done.16, f16[256,2048]{1,0:T(8,128)(2,1)} %collective-permute-done, f16[256,2048]{1,0:T(8,128)(2,1)} %convolution_convert_fusion.9, f32[2048]{0:T(1024)S(1)} %broadcast_multiply_fusion, ...), kind=kLoop, calls=%fused_computation.127 | loop fusion | flops 10485758 | bytes 6307840
  291.9 5.3 %constant_dynamic-update-slice_fusion.3 = (bf16[1280,2048]{1,0:T(8,128)(2,1)}, bf16[1280,2048]{1,0:T(8,128)(2,1)}) fusion(bf16[1280,2048]{1,0:T(8,128)(2,1)} %get-tuple-element.62, f32[2048]{0:T(1024)S(1)} %copy-done.16, f16[256,2048]{1,0:T(8,128)(2,1)} %collective-permute-done.11, f16[256,2048]{1,0:T(8,128)(2,1)} %convolution_convert_fusion.6, ...), kind=kLoop, calls=%fused_computation.126 | loop fusion | flops 10485760 | bytes 6307840
  298.3 4.3 %convolution_convert_fusion = bf16[256,2048]{1,0:T(8,128)(2,1)S(1)} fusion(bf16[2048,2304]{1,0:T(8,128)(2,1)S(1)} %bitcast.22, bf16[128,2304]{1,0:T(8,128)(2,1)} %get-tuple-element.25, bf16[128,2304]{1,0:T(8,128)(2,1)S(1)} %get-tuple-element.27), kind=kOutput, calls=%fused_computation.13 | convolution fusion | flops 2418802688 | bytes 11665408 | tf_op jit(solution)/shard_map/dot_general | solution.py:121
  308.1 5.2 %constant_dynamic-update-slice_fusion.1 = (bf16[1280,2048]{1,0:T(8,128)(2,1)}, bf16[1280,2048]{1,0:T(8,128)(2,1)}) fusion(bf16[1280,2048]{1,0:T(8,128)(2,1)} %get-tuple-element.58, f32[2048]{0:T(1024)S(1)} %copy-done.16, f16[256,2048]{1,0:T(8,128)(2,1)S(1)} %copy-done.9, f16[256,2048]{1,0:T(8,128)(2,1)S(1)} %copy-done.5, ...), kind=kLoop, calls=%fused_computation.124 | loop fusion | flops 10485760 | bytes 6307840
  313.4 14.8 %collective-permute-done.60 = bf16[256,2048]{1,0:T(8,128)(2,1)S(1)} collective-permute-done((bf16[256,2048]{1,0:T(8,128)(2,1)S(1)}, bf16[256,2048]{1,0:T(8,128)(2,1)S(1)}, u32[]{:S(2)}, u32[]{:S(2)}) %collective-permute-start.60) | collective-permute-done | bytes 1048608 | tf_op jit(solution)/shard_map/ppermute | solution.py:31
  331.7 18.7 %convolution_bitcast_fusion = f32[2304,2048]{0,1:T(8,128)} fusion(bf16[1280,2048]{1,0:T(8,128)(2,1)} %get-tuple-element.55, bf16[1280,2304]{1,0:T(8,128)(2,1)S(1)} %bitcast.26), kind=kOutput, calls=%fused_computation.4 | convolution fusion | flops 12079595520 | bytes 30015488 | tf_op jit(solution)/shard_map/dot_general | solution.py:149
  350.4 18.6 %copy.9 = f32[2304,2048]{1,0:T(8,128)} copy(f32[2304,2048]{0,1:T(8,128)} %convolution_bitcast_fusion) | data formatting | bytes 37748736
  369.0 6.9 %convert_reduce_fusion.1 = (f32[2048]{0:T(1024)S(1)}, f32[2048]{0:T(1024)}) fusion(bf16[1280,2048]{1,0:T(8,128)(2,1)} %get-tuple-element.54, bf16[1280,2048]{1,0:T(8,128)(2,1)} %get-tuple-element.55), kind=kLoop, calls=%fused_computation.6 | loop fusion | flops 10481664 | bytes 10502144 | tf_op jit(solution)/shard_map/reduce_sum | solution.py:137
  375.9 21.8 %fusion.1 = f32[2048,2304]{1,0:T(8,128)} fusion(bf16[2048,2304]{1,0:T(8,128)(2,1)} %param.8, bf16[1280,2048]{1,0:T(8,128)(2,1)} %get-tuple-element.54, bf16[1280,2304]{1,0:T(8,128)(2,1)} %copy-done.1, f32[2048]{0:T(1024)S(1)} %multiply_divide_fusion), kind=kOutput, calls=%fused_computation.3 | convolution fusion | flops 12093751296 | bytes 39460864 | tf_op jit(solution)/shard_map/dot_general | solution.py:138
  (254 shorter events, 159.3 us)
Async XLA Ops:
  8.4 27.4 %collective-permute-start = (f16[256,2048]{1,0:T(8,128)(2,1)}, f16[256,2048]{1,0:T(8,128)(2,1)}, u32[]{:S(2)}, u32[]{:S(2)}) collective-permute-start(f16[256,2048]{1,0:T(8,128)(2,1)} %convolution_convert_fusion.9), channel_id=1, source_target_pairs={{0,16},{16,0},{1,17},{17,1},{2,18},{18,2},{3,19},{19,3},{4,20},{20... | collective-permute-start | bytes 3145736 | tf_op jit(solution)/shard_map/ppermute | solution.py:31
  13.3 22.5 %collective-permute-start.14 = (f32[2048]{0:T(1024)S(1)}, f32[2048]{0:T(1024)S(1)}, u32[]{:S(2)}, u32[]{:S(2)}) collective-permute-start(f32[2048]{0:T(1024)S(1)} %fusion), channel_id=1, source_target_pairs={{0,16},{16,0},{1,17},{17,1},{2,18},{18,2},{3,19},{19,3},{4,20},{20... | collective-permute-start | bytes 24584 | tf_op jit(solution)/shard_map/ppermute | solution.py:31
  21.2 36.3 %collective-permute-start.11 = (f16[256,2048]{1,0:T(8,128)(2,1)}, f16[256,2048]{1,0:T(8,128)(2,1)}, u32[]{:S(2)}, u32[]{:S(2)}) collective-permute-start(f16[256,2048]{1,0:T(8,128)(2,1)} %convolution_convert_fusion.6), channel_id=1, source_target_pairs={{0,16},{16,0},{1,17},{17,1},{2,18},{18,2},{3,19},{19,3},{4,20},{20... | collective-permute-start | bytes 3145736 | tf_op jit(solution)/shard_map/ppermute | solution.py:31
  43.9 81.4 %collective-permute-start.1 = (f32[128,2304]{1,0:T(8,128)S(1)}, f32[128,2304]{1,0:T(8,128)S(1)}, u32[]{:S(2)}, u32[]{:S(2)}) collective-permute-start(f32[128,2304]{1,0:T(8,128)S(1)} %constant_dynamic-slice_fusion.4), channel_id=1, source_target_pairs={{0,1},{1,0},{2,3},{3,2},{4,5},{5,4},{6,7},{7,6},{8,9},{9,8},{10,11... | collective-permute-start | bytes 3538952 | tf_op jit(solution)/shard_map/ppermute | solution.py:24
  57.5 52.2 %collective-permute-start.12 = (f16[256,2048]{1,0:T(8,128)(2,1)S(1)}, f16[256,2048]{1,0:T(8,128)(2,1)S(1)}, u32[]{:S(2)}, u32[]{:S(2)}) collective-permute-start(f16[256,2048]{1,0:T(8,128)(2,1)S(1)} %convolution_convert_fusion.7), channel_id=1, source_target_pairs={{0,16},{16,0},{1,17},{17,1},{2,18},{18,2},{3,19},{19,3},{4,20},{20... | collective-permute-start | bytes 3145736 | tf_op jit(solution)/shard_map/ppermute | solution.py:31
  59.2 45.1 %collective-permute-start.25 = (f16[256,2048]{1,0:T(8,128)(2,1)S(1)}, f16[256,2048]{1,0:T(8,128)(2,1)S(1)}, u32[]{:S(2)}, u32[]{:S(2)}) collective-permute-start(f16[256,2048]{1,0:T(8,128)(2,1)S(1)} %convolution_convert_fusion.3), channel_id=1, source_target_pairs={{0,16},{16,0},{1,17},{17,1},{2,18},{18,2},{3,19},{19,3},{4,20},{20... | collective-permute-start | bytes 3145736 | tf_op jit(solution)/shard_map/ppermute | solution.py:31
  67.6 59.4 %collective-permute-start.15 = (f32[128,2304]{1,0:T(8,128)S(1)}, f32[128,2304]{1,0:T(8,128)S(1)}, u32[]{:S(2)}, u32[]{:S(2)}) collective-permute-start(f32[128,2304]{1,0:T(8,128)S(1)} %constant_dynamic-slice_fusion.3), channel_id=1, source_target_pairs={{0,1},{1,0},{2,3},{3,2},{4,5},{5,4},{6,7},{7,6},{8,9},{9,8},{10,11... | collective-permute-start | bytes 3538952 | tf_op jit(solution)/shard_map/ppermute | solution.py:24
  104.3 77.2 %collective-permute-start.26 = (f16[256,2048]{1,0:T(8,128)(2,1)S(1)}, f16[256,2048]{1,0:T(8,128)(2,1)S(1)}, u32[]{:S(2)}, u32[]{:S(2)}) collective-permute-start(f16[256,2048]{1,0:T(8,128)(2,1)S(1)} %convolution_convert_fusion.4), channel_id=1, source_target_pairs={{0,16},{16,0},{1,17},{17,1},{2,18},{18,2},{3,19},{19,3},{4,20},{20... | collective-permute-start | bytes 3145736 | tf_op jit(solution)/shard_map/ppermute | solution.py:31
  109.6 76.3 %collective-permute-start.28 = (f32[128,2304]{1,0:T(8,128)S(1)}, f32[128,2304]{1,0:T(8,128)S(1)}, u32[]{:S(2)}, u32[]{:S(2)}) collective-permute-start(f32[128,2304]{1,0:T(8,128)S(1)} %constant_dynamic-slice_fusion.2), channel_id=1, source_target_pairs={{0,1},{1,0},{2,3},{3,2},{4,5},{5,4},{6,7},{7,6},{8,9},{9,8},{10,11... | collective-permute-start | bytes 3538952 | tf_op jit(solution)/shard_map/ppermute | solution.py:24
  125.5 9.9 %collective-permute-start.2 = (bf16[64,2304]{1,0:T(8,128)(2,1)S(1)}, bf16[64,2304]{1,0:T(8,128)(2,1)S(1)}, u32[]{:S(2)}, u32[]{:S(2)}) collective-permute-start(bf16[64,2304]{1,0:T(8,128)(2,1)S(1)} %dynamic-slice_convert_fusion.4), channel_id=1, source_target_pairs={{0,2},{1,3},{2,0},{3,1},{4,6},{5,7},{6,4},{7,5},{8,10},{9,11},{10,... | collective-permute-start | bytes 884744 | tf_op jit(solution)/shard_map/ppermute | solution.py:24
  127.3 14.0 %collective-permute-start.16 = (bf16[64,2304]{1,0:T(8,128)(2,1)S(1)}, bf16[64,2304]{1,0:T(8,128)(2,1)S(1)}, u32[]{:S(2)}, u32[]{:S(2)}) collective-permute-start(bf16[64,2304]{1,0:T(8,128)(2,1)S(1)} %dynamic-slice_convert_fusion.3), channel_id=1, source_target_pairs={{0,2},{1,3},{2,0},{3,1},{4,6},{5,7},{6,4},{7,5},{8,10},{9,11},{10,... | collective-permute-start | bytes 884744 | tf_op jit(solution)/shard_map/ppermute | solution.py:24
  148.9 39.5 %collective-permute-start.39 = (f32[128,2304]{1,0:T(8,128)S(1)}, f32[128,2304]{1,0:T(8,128)S(1)}, u32[]{:S(2)}, u32[]{:S(2)}) collective-permute-start(f32[128,2304]{1,0:T(8,128)S(1)} %constant_dynamic-slice_fusion.1), channel_id=1, source_target_pairs={{0,1},{1,0},{2,3},{3,2},{4,5},{5,4},{6,7},{7,6},{8,9},{9,8},{10,11... | collective-permute-start | bytes 3538952 | tf_op jit(solution)/shard_map/ppermute | solution.py:24
  177.5 12.4 %collective-permute-start.10 = (bf16[128,2304]{1,0:T(8,128)(2,1)S(1)}, bf16[128,2304]{1,0:T(8,128)(2,1)S(1)}, u32[]{:S(2)}, u32[]{:S(2)}) collective-permute-start(bf16[128,2304]{1,0:T(8,128)(2,1)S(1)} %pad_maximum_fusion), channel_id=1, source_target_pairs={{0,1},{1,0},{2,3},{3,2},{4,5},{5,4},{6,7},{7,6},{8,9},{9,8},{10,11... | collective-permute-start | bytes 1769480 | tf_op jit(solution)/shard_map/ppermute | solution.py:24
  181.5 15.7 %collective-permute-start.24 = (bf16[128,2304]{1,0:T(8,128)(2,1)}, bf16[128,2304]{1,0:T(8,128)(2,1)S(1)}, u32[]{:S(2)}, u32[]{:S(2)}) collective-permute-start(bf16[128,2304]{1,0:T(8,128)(2,1)} %pad_maximum_fusion.1), channel_id=1, source_target_pairs={{0,1},{1,0},{2,3},{3,2},{4,5},{5,4},{6,7},{7,6},{8,9},{9,8},{10,11... | collective-permute-start | bytes 1769480 | tf_op jit(solution)/shard_map/ppermute | solution.py:24
  185.4 63.3 %collective-permute-start.50 = (f32[128,2304]{1,0:T(8,128)S(1)}, f32[128,2304]{1,0:T(8,128)}, u32[]{:S(2)}, u32[]{:S(2)}) collective-permute-start(f32[128,2304]{1,0:T(8,128)S(1)} %constant_dynamic-slice_fusion), channel_id=1, source_target_pairs={{0,1},{1,0},{2,3},{3,2},{4,5},{5,4},{6,7},{7,6},{8,9},{9,8},{10,11... | collective-permute-start | bytes 3538952 | tf_op jit(solution)/shard_map/ppermute | solution.py:24
  186.9 17.1 %collective-permute-start.29 = (bf16[64,2304]{1,0:T(8,128)(2,1)}, bf16[64,2304]{1,0:T(8,128)(2,1)}, u32[]{:S(2)}, u32[]{:S(2)}) collective-permute-start(bf16[64,2304]{1,0:T(8,128)(2,1)} %dynamic-slice_convert_fusion.2), channel_id=1, source_target_pairs={{0,2},{1,3},{2,0},{3,1},{4,6},{5,7},{6,4},{7,5},{8,10},{9,11},{10,... | collective-permute-start | bytes 884744 | tf_op jit(solution)/shard_map/ppermute | solution.py:24
  189.4 18.4 %collective-permute-start.40 = (bf16[64,2304]{1,0:T(8,128)(2,1)}, bf16[64,2304]{1,0:T(8,128)(2,1)}, u32[]{:S(2)}, u32[]{:S(2)}) collective-permute-start(bf16[64,2304]{1,0:T(8,128)(2,1)} %dynamic-slice_convert_fusion.1), channel_id=1, source_target_pairs={{0,2},{1,3},{2,0},{3,1},{4,6},{5,7},{6,4},{7,5},{8,10},{9,11},{10,... | collective-permute-start | bytes 884744 | tf_op jit(solution)/shard_map/ppermute | solution.py:24
  196.7 58.0 %collective-permute-start.13 = (bf16[256,2048]{1,0:T(8,128)(2,1)}, bf16[256,2048]{1,0:T(8,128)(2,1)}, u32[]{:S(2)}, u32[]{:S(2)}) collective-permute-start(bf16[256,2048]{1,0:T(8,128)(2,1)} %convolution_convert_fusion.8), channel_id=1, source_target_pairs={{0,16},{16,0},{1,17},{17,1},{2,18},{18,2},{3,19},{19,3},{4,20},{20... | collective-permute-start | bytes 3145736 | tf_op jit(solution)/shard_map/ppermute | solution.py:31
  217.5 57.6 %collective-permute-start.27 = (bf16[256,2048]{1,0:T(8,128)(2,1)}, bf16[256,2048]{1,0:T(8,128)(2,1)S(1)}, u32[]{:S(2)}, u32[]{:S(2)}) collective-permute-start(bf16[256,2048]{1,0:T(8,128)(2,1)} %convolution_convert_fusion.5), channel_id=1, source_target_pairs={{0,16},{16,0},{1,17},{17,1},{2,18},{18,2},{3,19},{19,3},{4,20},{20... | collective-permute-start | bytes 3145736 | tf_op jit(solution)/shard_map/ppermute | solution.py:31
  250.2 9.5 %collective-permute-start.51 = (bf16[64,2304]{1,0:T(8,128)(2,1)S(1)}, bf16[64,2304]{1,0:T(8,128)(2,1)S(1)}, u32[]{:S(2)}, u32[]{:S(2)}) collective-permute-start(bf16[64,2304]{1,0:T(8,128)(2,1)S(1)} %dynamic-slice_convert_fusion), channel_id=1, source_target_pairs={{0,2},{1,3},{2,0},{3,1},{4,6},{5,7},{6,4},{7,5},{8,10},{9,11},{10,... | collective-permute-start | bytes 884744 | tf_op jit(solution)/shard_map/ppermute | solution.py:24
  254.7 47.9 %collective-permute-start.38 = (bf16[256,2048]{1,0:T(8,128)(2,1)S(1)}, bf16[256,2048]{1,0:T(8,128)(2,1)S(1)}, u32[]{:S(2)}, u32[]{:S(2)}) collective-permute-start(bf16[256,2048]{1,0:T(8,128)(2,1)S(1)} %convolution_convert_fusion.2), channel_id=1, source_target_pairs={{0,16},{16,0},{1,17},{17,1},{2,18},{18,2},{3,19},{19,3},{4,20},{20... | collective-permute-start | bytes 3145736 | tf_op jit(solution)/shard_map/ppermute | solution.py:31
  271.1 10.1 %collective-permute-start.55 = (bf16[16,2304]{1,0:T(8,128)(2,1)S(1)}, bf16[16,2304]{1,0:T(8,128)(2,1)S(1)}, u32[]{:S(2)}, u32[]{:S(2)}) collective-permute-start(bf16[16,2304]{1,0:T(8,128)(2,1)S(1)} %get-tuple-element.45), channel_id=1, source_target_pairs={{0,4},{1,5},{2,6},{3,7},{4,8},{5,9},{6,10},{7,11},{8,12},{9,13},{1... | collective-permute-start | bytes 221192 | tf_op jit(solution)/shard_map/ppermute | solution.py:28
  275.1 33.0 %collective-permute-start.49 = (bf16[256,2048]{1,0:T(8,128)(2,1)S(1)}, bf16[256,2048]{1,0:T(8,128)(2,1)}, u32[]{:S(2)}, u32[]{:S(2)}) collective-permute-start(bf16[256,2048]{1,0:T(8,128)(2,1)S(1)} %convolution_convert_fusion.1), channel_id=1, source_target_pairs={{0,16},{16,0},{1,17},{17,1},{2,18},{18,2},{3,19},{19,3},{4,20},{20... | collective-permute-start | bytes 3145736 | tf_op jit(solution)/shard_map/ppermute | solution.py:31
  302.6 25.6 %collective-permute-start.60 = (bf16[256,2048]{1,0:T(8,128)(2,1)S(1)}, bf16[256,2048]{1,0:T(8,128)(2,1)S(1)}, u32[]{:S(2)}, u32[]{:S(2)}) collective-permute-start(bf16[256,2048]{1,0:T(8,128)(2,1)S(1)} %convolution_convert_fusion), channel_id=1, source_target_pairs={{0,16},{16,0},{1,17},{17,1},{2,18},{18,2},{3,19},{19,3},{4,20},{20... | collective-permute-start | bytes 3145736 | tf_op jit(solution)/shard_map/ppermute | solution.py:31
  (64 other events, 955.0 us)

commit v2 on v0

v2 whole, which is shorter than its diff:
```python
import functools

import jax
import jax.numpy as jnp
import numpy as np
from jax import lax
from jax.experimental import pallas as pl
from jax.experimental.pallas import tpu as pltpu
from jax.sharding import PartitionSpec as P

OVER_ROWS = (((0,), (0,)), ((), ()))
OVER_COLUMNS = (((1,), (1,)), ((), ()))
WIRE = jnp.bfloat16
PARAMS = pltpu.CompilerParams(vmem_limit_bytes=44 * 2**20)


def split_rows(rows):
    for parts in (5, 4, 2):
        if rows % (parts * 64) == 0:
            return parts
    return 1


def block_of(size, least=256):
    return least if size % least == 0 else size


def softplus(x):
    return jnp.maximum(x, 0.0) + jnp.log1p(jnp.exp(-jnp.abs(x)))


def delta_of(own_back, other_back, own_pre, other_pre, bias, penalty):
    pre = own_pre.astype(jnp.float32) + other_pre.astype(jnp.float32) + bias
    back = own_back.astype(jnp.float32) + other_back.astype(jnp.float32) + penalty
    return (back * jax.nn.sigmoid(pre)).astype(jnp.bfloat16)


def slot_kernel(tasks, n_in, *refs):
    ins, outs = list(refs[:n_in]), list(refs[n_in:])
    if "send" in tasks:
        send_sem, recv_sem = outs.pop(-2), outs.pop(-1)
        payload, received = ins.pop(0), outs.pop(0)
        partner = {"layer": 1 - lax.axis_index("layer")}
        exchange = pltpu.make_async_remote_copy(
            src_ref=payload,
            dst_ref=received,
            send_sem=send_sem,
            recv_sem=recv_sem,
            device_id=partner,
            device_id_type=pl.DeviceIdType.MESH,
        )

        @pl.when(pl.program_id(0) == 0)
        def _():
            barrier = pltpu.get_barrier_semaphore()
            pl.semaphore_signal(
                barrier, inc=1, device_id=partner, device_id_type=pl.DeviceIdType.MESH
            )
            pl.semaphore_wait(barrier, 1)
            exchange.start()

    def take(count):
        taken = ins[:count]
        del ins[:count]
        return taken

    if "encode" in tasks:
        acts, weight = take(2)
        own = jnp.dot(acts[...], weight[...], preferred_element_type=jnp.float32)
        outs.pop(0)[...] = own.astype(WIRE)
    if "recon" in tasks or "back" in tasks:
        (dec,) = take(1)
    if "recon" in tasks:
        own_pre, other_pre, bias = take(3)
        pre = own_pre[...].astype(jnp.float32) + other_pre[...].astype(jnp.float32) + bias[...]
        codes = softplus(pre).astype(jnp.bfloat16)
        outs.pop(0)[...] = codes
        total = outs.pop(0)
        product = jnp.dot(codes, dec[...], preferred_element_type=jnp.float32)

        @pl.when(pl.program_id(0) == 0)
        def _():
            total[...] = product

        @pl.when(pl.program_id(0) > 0)
        def _():
            total[...] += product

    if "back" in tasks:
        (err,) = take(1)
        own = lax.dot_general(
            err[...], dec[...], OVER_COLUMNS, preferred_element_type=jnp.float32
        )
        outs.pop(0)[...] = own.astype(WIRE)
    if "delta" in tasks:
        values = [r[...] for r in take(6)]
        outs.pop(0)[...] = delta_of(*values)
    if "send" in tasks:

        @pl.when(pl.program_id(0) == pl.num_programs(0) - 1)
        def _():
            exchange.wait()


def run_slot(tasks, slot=0):
    if "encode" in tasks:
        part, latents = tasks["encode"][0].shape[0], tasks["encode"][1].shape[1]
    elif "recon" in tasks:
        part, latents = tasks["recon"][0].shape
    elif "back" in tasks:
        part, latents = tasks["back"][0].shape[0], tasks["dec"].shape[0]
    else:
        part, latents = tasks["delta"][0].shape
    width = tasks["dec"].shape[1]
    block = block_of(latents, 512)
    tile = pl.BlockSpec((part, block), lambda j: (0, j))
    line = pl.BlockSpec((1, block), lambda j: (0, j))
    whole = pl.BlockSpec((part, width), lambda j: (0, 0))
    operands, in_specs, shapes, out_specs, names = [], [], [], [], []
    flops = 0
    if "send" in tasks:
        operands.append(tasks["send"])
        in_specs.append(pl.BlockSpec(memory_space=pl.ANY))
        shapes.append(jax.ShapeDtypeStruct(tasks["send"].shape, tasks["send"].dtype))
        out_specs.append(pl.BlockSpec(memory_space=pl.ANY))
        names.append("received")
    if "encode" in tasks:
        operands += tasks["encode"]
        in_specs += [whole, pl.BlockSpec((width, block), lambda j: (0, j))]
        shapes.append(jax.ShapeDtypeStruct((part, latents), WIRE))
        out_specs.append(tile)
        names.append("encode")
        flops += 2 * part * width * latents
    if "recon" in tasks or "back" in tasks:
        operands.append(tasks["dec"])
        in_specs.append(pl.BlockSpec((block, width), lambda j: (j, 0)))
    if "recon" in tasks:
        operands += tasks["recon"]
        in_specs += [tile, tile, line]
        shapes.append(jax.ShapeDtypeStruct((part, latents), jnp.bfloat16))
        shapes.append(jax.ShapeDtypeStruct((part, width), jnp.float32))
        out_specs += [tile, whole]
        names += ["codes", "partial"]
        flops += 2 * part * width * latents
    if "back" in tasks:
        operands += tasks["back"]
        in_specs.append(whole)
        shapes.append(jax.ShapeDtypeStruct((part, latents), WIRE))
        out_specs.append(tile)
        names.append("back")
        flops += 2 * part * width * latents
    if "delta" in tasks:
        operands += tasks["delta"]
        in_specs += [tile, tile, tile, tile, line, line]
        shapes.append(jax.ShapeDtypeStruct((part, latents), jnp.bfloat16))
        out_specs.append(tile)
        names.append("delta")
    outs = pl.pallas_call(
        functools.partial(slot_kernel, tuple(tasks), len(operands)),
        grid=(latents // block,),
        out_shape=tuple(shapes),
        in_specs=in_specs,
        out_specs=tuple(out_specs),
        scratch_shapes=[pltpu.SemaphoreType.DMA] * 2 if "send" in tasks else [],
        compiler_params=pltpu.CompilerParams(
            vmem_limit_bytes=44 * 2**20, collective_id=slot, has_side_effects=True
        )
        if "send" in tasks
        else PARAMS,
        cost_estimate=pl.CostEstimate(
            flops=flops, bytes_accessed=4 * width * latents, transcendentals=2 * part * latents
        ),
    )(*operands)
    return dict(zip(names, outs))


def error_kernel(factor, total_ref, bias_ref, acts_ref, out_ref):
    err = factor * (total_ref[...] + bias_ref[...] - acts_ref[...].astype(jnp.float32))
    out_ref[...] = err.astype(jnp.bfloat16)


def error_of(factor, total, bias, acts):
    return pl.pallas_call(
        functools.partial(error_kernel, factor),
        out_shape=jax.ShapeDtypeStruct(total.shape, jnp.bfloat16),
    )(total, bias, acts)


def grad_dec_kernel(parts, *refs):
    codes, errs = refs[:parts], refs[parts : 2 * parts]
    coef_ref, dec_ref, out_ref = refs[2 * parts :]
    total = coef_ref[...] * dec_ref[...].astype(jnp.float32)
    code = jnp.concatenate([c[...] for c in codes], axis=0)
    err = jnp.concatenate([e[...] for e in errs], axis=0)
    out_ref[...] = total + lax.dot_general(
        code, err, OVER_ROWS, preferred_element_type=jnp.float32
    )


def grad_dec_of(codes, errs, coef, dec):
    part, latents = codes[0].shape
    width = errs[0].shape[1]
    block = block_of(latents)
    parts = len(codes)
    return pl.pallas_call(
        functools.partial(grad_dec_kernel, parts),
        grid=(latents // block,),
        out_shape=jax.ShapeDtypeStruct((latents, width), jnp.float32),
        in_specs=[pl.BlockSpec((part, block), lambda i: (0, i))] * parts
        + [pl.BlockSpec((part, width), lambda i: (0, 0))] * parts
        + [
            pl.BlockSpec((block, 1), lambda i: (i, 0)),
            pl.BlockSpec((block, width), lambda i: (i, 0)),
        ],
        out_specs=pl.BlockSpec((block, width), lambda i: (i, 0)),
        compiler_params=PARAMS,
        cost_estimate=pl.CostEstimate(
            flops=2 * parts * part * latents * width,
            bytes_accessed=latents * width * 6,
            transcendentals=0,
        ),
    )(*codes, *errs, coef, dec)


def grad_enc_kernel(parts, *refs):
    acts_ref, deltas = refs[0], refs[1 : parts + 1]
    out_ref, bias_ref = refs[parts + 1 :]

    @pl.when(pl.program_id(0) == 0)
    def _():
        total = jnp.zeros_like(bias_ref)
        for d in deltas:
            total += jnp.sum(d[...].astype(jnp.float32), axis=0, keepdims=True)
        bias_ref[...] = total

    delta = jnp.concatenate([d[...] for d in deltas], axis=0)
    out_ref[...] = lax.dot_general(
        acts_ref[...], delta, OVER_ROWS, preferred_element_type=jnp.float32
    )


def grad_enc_of(acts, deltas):
    rows, width = acts.shape
    part, latents = deltas[0].shape
    parts = len(deltas)
    block = block_of(width)
    return pl.pallas_call(
        functools.partial(grad_enc_kernel, parts),
        grid=(width // block,),
        out_shape=(
            jax.ShapeDtypeStruct((width, latents), jnp.float32),
            jax.ShapeDtypeStruct((1, latents), jnp.float32),
        ),
        in_specs=[pl.BlockSpec((rows, block), lambda i: (0, i))]
        + [pl.BlockSpec((part, latents), lambda i: (0, 0))] * parts,
        out_specs=(
            pl.BlockSpec((block, latents), lambda i: (i, 0)),
            pl.BlockSpec((1, latents), lambda i: (0, 0)),
        ),
        compiler_params=PARAMS,
        cost_estimate=pl.CostEstimate(
            flops=2 * rows * latents * width,
            bytes_accessed=latents * width * 4,
            transcendentals=0,
        ),
    )(acts, *deltas)


def make_per_device(n_layer, n_latent):
    def other_layer(array):
        if n_layer == 2:
            return lax.ppermute(array, "layer", [(0, 1), (1, 0)])
        wide = array.astype(jnp.float32)
        return lax.psum(wide, "layer") - wide

    def per_device(acts, enc_weight, enc_bias, dec_weight, dec_bias):
        rows = acts.shape[0]
        n = split_rows(rows)
        part = rows // n
        piece = part // n_latent
        scale = 1.0 / jnp.sqrt(jnp.float32(rows))
        factor = float(np.float32(2.0) * (np.float32(1.0) / np.sqrt(np.float32(rows))))
        sparsity = 1.0
        index = lax.axis_index("latent")
        bias = enc_bias[None, :]

        def after(array, earlier):
            return lax.optimization_barrier((array, earlier))[0]

        def acts_of(k):
            return acts[k * part : (k + 1) * part]

        dec_f = dec_weight.astype(jnp.float32)
        squares = jnp.sum(dec_f * dec_f, axis=1)
        norms = jnp.sqrt(squares + other_layer(squares) + 1e-06)
        penalty = (sparsity * scale * norms)[None, :]

        own_pre, other_pre, codes, partials, scattered, errs = {}, {}, {}, {}, {}, {}
        own_back, other_back, deltas = {}, {}, {}
        own_pre[0] = run_slot({"encode": (acts_of(0), enc_weight), "dec": dec_weight})["encode"]

        for s in range(2 * n - 1):
            payload = own_pre[s] if s < n else own_back[s - n]
            if 0 <= s - 3 < n:
                total = after(scattered[s - 3], payload)
                start = (s - 3) * part + index * piece
                mine = lax.dynamic_slice_in_dim(acts, start, piece, axis=0)
                err = error_of(factor, total, dec_bias[None, :], mine)
                errs[s - 3] = lax.all_gather(err, "latent", tiled=True)
            tasks = {"dec": dec_weight}
            if n_layer == 2:
                tasks["send"] = payload
            if s + 1 < n:
                tasks["encode"] = (after(acts_of(s + 1), payload), enc_weight)
            if 0 <= s - 1 < n:
                tasks["recon"] = (own_pre[s - 1], after(other_pre[s - 1], payload), bias)
            if 0 <= s - (n - 1) < n:
                tasks["back"] = (after(errs[s - (n - 1)], payload),)
            if 0 <= s - n - 1:
                k = s - n - 1
                tasks["delta"] = (
                    own_back[k], after(other_back[k], payload), own_pre[k], other_pre[k], bias, penalty
                )
            outs = run_slot(tasks, s)
            received = outs["received"] if n_layer == 2 else other_layer(payload)
            if s < n:
                other_pre[s] = received
            else:
                other_back[s - n] = received
            if "encode" in outs:
                own_pre[s + 1] = outs["encode"]
            if "partial" in outs:
                codes[s - 1], partials[s - 1] = outs["codes"], outs["partial"]
                scattered[s - 1] = lax.psum_scatter(
                    outs["partial"], "latent", scatter_dimension=0, tiled=True
                )
            if "back" in outs:
                own_back[s - (n - 1)] = outs["back"]
            if "delta" in outs:
                deltas[s - n - 1] = outs["delta"]

        payload = own_back[n - 1]
        other_back[n - 1] = other_layer(payload)
        column = sum(jnp.sum(codes[k].astype(jnp.float32), axis=0) for k in range(n))
        grad_dec_bias = sum(jnp.sum(errs[k].astype(jnp.float32), axis=0) for k in range(n))
        coef = after((sparsity * scale * column / norms)[:, None], payload)
        grad_dec = grad_dec_of(
            [codes[k] for k in range(n)], [errs[k] for k in range(n)], coef, dec_weight
        )
        other_back[n - 1] = after(other_back[n - 1], grad_dec)
        for k in range(n):
            if k not in deltas:
                tasks = {"dec": dec_weight}
                tasks["delta"] = (
                    own_back[k], other_back[k], own_pre[k], other_pre[k], bias, penalty
                )
                deltas[k] = run_slot(tasks)["delta"]
        grad_enc, grad_enc_bias = grad_enc_of(acts, [deltas[k] for k in range(n)])
        return (grad_enc, grad_enc_bias[0], grad_dec, grad_dec_bias)

    return per_device


def solution(mesh):
    return jax.shard_map(
        make_per_device(mesh.shape["layer"], mesh.shape["latent"]),
        mesh=mesh,
        in_specs=(
            P(None, "layer"),
            P("layer", "latent"),
            P("latent"),
            P("latent", "layer"),
            P("layer"),
        ),
        out_specs=(P("layer", "latent"), P("latent"), P("latent", "layer"), P("layer")),
        check_vma=False,
    )
```

time: 849 us -> 704 us (0.83)
  waiting for transfers between devices: 679 us -> 293 us
  Pallas kernels: 0 us -> 298 us
  matrix products: 94.3 us -> 0 us
  local copies, waits for them, and re-layouts: 20.9 us -> 79 us
  other arithmetic: 35.3 us -> 13.3 us
    psum x3 -> x0, waiting for transfers between devices: 679 us -> none  [the longest x1 246 us: per_device(): summed_pre, summed_sq = lax.psum((partial_pre, squares), 'layer')]
    pallas_call x0 -> x19, Pallas kernels: none -> 298 us  [the longest x12 253 us: run_slot(): pl.pallas_call(functools.partial(slot_kernel, tuple(tasks), len(operands)...]
    reduce_scatter x0 -> x5, waiting for transfers between devices: none -> 149 us  [per_device(): lax.psum_scatter(outs['partial'], 'latent', scatter_dimension=0, tiled=True)]
    all_gather x0 -> x5, waiting for transfers between devices: none -> 143 us  [per_device(): errs[s - 3] = lax.all_gather(err, 'latent', tiled=True)]
    dot_general x5 -> x0, matrix products: 94.3 us -> none  [the longest x1 21.6 us: per_device(): lax.dot_general(codes, err_grad, (((0,), (0,)), ((), ())), preferred_elem...]
    unnamed x7 -> x162, local copies, waits for them, and re-layouts: 20.9 us -> 70.7 us
    reduce_sum x3 -> x10, other arithmetic: 29.7 us -> 6.98 us  [the longest x5 6.13 us: per_device(): jnp.sum(errs[k].astype(jnp.float32), axis=0)]
  transfers between devices with their start and end apart: 3 -> 12, of which waited for: 3 -> 11; matrix products, arithmetic and copies ran while one was open for 3% -> 2% of each run, Pallas kernels for 0% -> 27%
where the time goes in v2:
time: 704 us; the launch traced here: 702 us
  Pallas kernels  298 us (42%)
  waiting for transfers between devices  293 us (42%)
  local copies, waits for them, and re-layouts  79 us (11%)
  between operations  14.6 us (2%)
  other arithmetic  13.3 us (2%)
    pallas_call x12, Pallas kernels, run_slot(): pl.pallas_call(functools.partial(slot_kernel, tuple(tasks), len(operands)...  253 us
    reduce_scatter x5, waiting for transfers between devices, per_device(): lax.psum_scatter(outs['partial'], 'latent', scatter_dimension=0, tiled=True)  149 us
    all_gather x5, waiting for transfers between devices, per_device(): errs[s - 3] = lax.all_gather(err, 'latent', tiled=True)  143 us
    unnamed x162, local copies, waits for them, and re-layouts  70.7 us
    pallas_call x1, Pallas kernels, grad_dec_of(): pl.pallas_call(functools.partial(grad_dec_kernel, parts), grid=(latents /...  18.9 us
    pallas_call x1, Pallas kernels, grad_enc_of(): pl.pallas_call(functools.partial(grad_enc_kernel, parts), grid=(width //...  17.5 us
  transfers between devices with their start and end apart: 12, of which 11 were waited for; matrix products, arithmetic and copies ran while one was open for 2% of the time, Pallas kernels for 27%

profile of v2, /device:TPU:0, one launch (start us, length us, event | category | flops | bytes accessed | tf_op | source)
XLA Modules:
  0.0 701.6 jit_solution(3203683751468207937)
XLA Ops:
  7.2 4.5 fusion
  11.7 5.9 shard_map.84.refs_0_.refs_4_.refs_5_
  17.6 27.9 %shard_map.85 = (bf16[256,2048]{1,0:T(8,128)(2,1)S(1)}, bf16[256,2048]{1,0:T(8,128)(2,1)S(1)}) custom-call(bf16[256,2048]{1,0:T(8,128)(2,1)S(1)} %shard_map.84.refs_0_.refs_4_.refs_5_, bf16[256,2304]{1,0:T(8,128)(2,1)S(1)} %get-tuple-element.61.refs_1_, bf16[2304,2048]{1,0:T(8,128)(2,1)} %refs_2_.7), custom_call_target="tpu_custom_call" | custom-call | flops 2415919104 | bytes 18874368 | tf_op jit(solution)/shard_map/pallas_call | solution.py:158
  45.5 27.2 %shard_map.86 = (bf16[256,2048]{1,0:T(8,128)(2,1)S(1)}, bf16[256,2048]{1,0:T(8,128)(2,1)S(1)}, bf16[256,2048]{1,0:T(8,128)(2,1)S(1)}, f32[256,2304]{1,0:T(8,128)S(1)}) custom-call(bf16[256,2048]{1,0:T(8,128)(2,1)S(1)} %get-tuple-element.62.refs_0_.refs_4_.refs_5_, bf16[256,2304]{1,0:T(8,128)(2,1)S(1)} %get-tuple-element.63.refs_1_, ...), custom_call_target="tpu_custom_call" | custom-call | flops 4831838208 | bytes 18874368 | tf_op jit(solution)/shard_map/pallas_call | solution.py:158
  78.6 25.9 %shard_map.87 = (bf16[256,2048]{1,0:T(8,128)(2,1)S(1)}, bf16[256,2048]{1,0:T(8,128)(2,1)S(1)}, bf16[256,2048]{1,0:T(8,128)(2,1)S(1)}, f32[256,2304]{1,0:T(8,128)S(1)}) custom-call(bf16[256,2048]{1,0:T(8,128)(2,1)S(1)} %get-tuple-element.65.refs_0_.refs_4_.refs_5_, bf16[256,2304]{1,0:T(8,128)(2,1)S(1)} %copy-done.6, bf16[2304,2048]{1,0:T(8,128)(2,1)} %refs_2_.7, ...), custom_call_target="tpu_custom_call" | custom-call | flops 4831838208 | bytes 18874368 | tf_op jit(solution)/shard_map/pallas_call | solution.py:158
  112.0 28.3 %reduce-scatter.6.cloned.1.call-done.total_ref = f32[16,2304]{1,0:T(8,128)} async-done(((f32[256,2304]{1,0:T(8,128)}), f32[16,2304]{1,0:T(8,128)}) %reduce-scatter.6.cloned.1.call-update) | async-done | bytes 147472 | tf_op jit(solution)/shard_map/reduce_scatter | solution.py:334
  145.8 25.8 %shard_map.88 = (bf16[256,2048]{1,0:T(8,128)(2,1)S(1)}, bf16[256,2048]{1,0:T(8,128)(2,1)S(1)}, bf16[256,2048]{1,0:T(8,128)(2,1)S(1)}, f32[256,2304]{1,0:T(8,128)S(1)}) custom-call(bf16[256,2048]{1,0:T(8,128)(2,1)S(1)} %copy-done.19, bf16[256,2304]{1,0:T(8,128)(2,1)S(1)} %copy-done.5, bf16[2304,2048]{1,0:T(8,128)(2,1)} %refs_2_.7, ...), custom_call_target="tpu_custom_call" | custom-call | flops 4831838208 | bytes 18874368 | tf_op jit(solution)/shard_map/pallas_call | solution.py:158
  176.1 31.1 %reduce-scatter.8.cloned.1.call-done.total_ref = f32[16,2304]{1,0:T(8,128)} async-done(((f32[256,2304]{1,0:T(8,128)}), f32[16,2304]{1,0:T(8,128)}) %reduce-scatter.8.cloned.1.call-update) | async-done | bytes 147472 | tf_op jit(solution)/shard_map/reduce_scatter | solution.py:334
  208.9 38.0 %all-gather.6.cloned.1.call-done.refs_5_ = bf16[256,2304]{1,0:T(8,128)(2,1)} async-done(((bf16[16,2304]{1,0:T(8,128)(2,1)}), bf16[256,2304]{1,0:T(8,128)(2,1)}) %all-gather.6.cloned.1.call-update) | async-done | bytes 1179664 | tf_op jit(solution)/shard_map/all_gather | solution.py:309
  251.8 27.1 %shard_map.90 = (bf16[256,2048]{1,0:T(8,128)(2,1)S(1)}, bf16[256,2048]{1,0:T(8,128)(2,1)S(1)}, f32[256,2304]{1,0:T(8,128)S(1)}, bf16[256,2048]{1,0:T(8,128)(2,1)S(1)}) custom-call(bf16[256,2048]{1,0:T(8,128)(2,1)S(1)} %copy-done.37, bf16[2048,2304]{1,0:T(8,128)(2,1)} %refs_11_.1, bf16[256,2048]{1,0:T(8,128)(2,1)S(1)} %copy-done.20, ...), custom_call_target="tpu_custom_call" | custom-call | flops 4831838208 | bytes 18874368 | tf_op jit(solution)/shard_map/pallas_call | solution.py:158
  283.3 29.7 %reduce-scatter.10.cloned.1.call-done.total_ref = f32[16,2304]{1,0:T(8,128)} async-done(((f32[256,2304]{1,0:T(8,128)}), f32[16,2304]{1,0:T(8,128)}) %reduce-scatter.10.cloned.1.call-update) | async-done | bytes 147472 | tf_op jit(solution)/shard_map/reduce_scatter | solution.py:334
  314.7 38.1 %all-gather.8.cloned.1.call-done.refs_5_.refs_6_ = bf16[256,2304]{1,0:T(8,128)(2,1)} async-done(((bf16[16,2304]{1,0:T(8,128)(2,1)}), bf16[256,2304]{1,0:T(8,128)(2,1)}) %all-gather.8.cloned.1.call-update) | async-done | bytes 1179664 | tf_op jit(solution)/shard_map/all_gather | solution.py:309
  357.7 27.1 %shard_map.92 = (bf16[256,2048]{1,0:T(8,128)(2,1)S(1)}, bf16[256,2048]{1,0:T(8,128)(2,1)S(1)}, f32[256,2304]{1,0:T(8,128)S(1)}, bf16[256,2048]{1,0:T(8,128)(2,1)S(1)}) custom-call(bf16[256,2048]{1,0:T(8,128)(2,1)S(1)} %copy-done.47, bf16[2048,2304]{1,0:T(8,128)(2,1)} %refs_11_.1, bf16[256,2048]{1,0:T(8,128)(2,1)S(1)} %copy-done.38, ...), custom_call_target="tpu_custom_call" | custom-call | flops 4831838208 | bytes 18874368 | tf_op jit(solution)/shard_map/pallas_call | solution.py:158
  389.2 30.2 %reduce-scatter.12.cloned.1.call-done.total_ref = f32[16,2304]{1,0:T(8,128)} async-done(((f32[256,2304]{1,0:T(8,128)}), f32[16,2304]{1,0:T(8,128)}) %reduce-scatter.12.cloned.1.call-update) | async-done | bytes 147472 | tf_op jit(solution)/shard_map/reduce_scatter | solution.py:334
  421.3 5.7 multiply_reduce_fusion
  430.8 28.3 %all-gather.10.cloned.1.call-done.refs_2_.refs_7_ = bf16[256,2304]{1,0:T(8,128)(2,1)} async-done(((bf16[16,2304]{1,0:T(8,128)(2,1)}), bf16[256,2304]{1,0:T(8,128)(2,1)}) %all-gather.10.cloned.1.call-update) | async-done | bytes 1179664 | tf_op jit(solution)/shard_map/all_gather | solution.py:309
  465.3 27.1 %shard_map.94 = (bf16[256,2048]{1,0:T(8,128)(2,1)S(1)}, bf16[256,2048]{1,0:T(8,128)(2,1)S(1)}, bf16[256,2048]{1,0:T(8,128)(2,1)S(1)}) custom-call(bf16[256,2048]{1,0:T(8,128)(2,1)S(1)} %copy-done.8, bf16[2048,2304]{1,0:T(8,128)(2,1)} %refs_11_.1, bf16[256,2304]{1,0:T(8,128)(2,1)S(1)} %copy-done, bf16[256,2048]{1,0:T(8,128)(2,1)S(1)} %copy-done.48, ...), custom_call_target="tpu_custom_call" | custom-call | flops 2415919104 | bytes 18874368 | tf_op jit(solution)/shard_map/pallas_call | solution.py:158
  495.3 30.1 %reduce-scatter.14.cloned.1.call-done.total_ref = f32[16,2304]{1,0:T(8,128)} async-done(((f32[256,2304]{1,0:T(8,128)}), f32[16,2304]{1,0:T(8,128)}) %reduce-scatter.14.cloned.1.call-update) | async-done | bytes 147472 | tf_op jit(solution)/shard_map/reduce_scatter | solution.py:334
  531.4 33.9 %all-gather.12.cloned.1.call-done.refs_2_.refs_8_ = bf16[256,2304]{1,0:T(8,128)(2,1)} async-done(((bf16[16,2304]{1,0:T(8,128)(2,1)}), bf16[256,2304]{1,0:T(8,128)(2,1)}) %all-gather.12.cloned.1.call-update) | async-done | bytes 1179664 | tf_op jit(solution)/shard_map/all_gather | solution.py:309
  570.3 27.1 %shard_map.96 = (bf16[256,2048]{1,0:T(8,128)(2,1)S(1)}, bf16[256,2048]{1,0:T(8,128)(2,1)S(1)}, bf16[256,2048]{1,0:T(8,128)(2,1)S(1)}) custom-call(bf16[256,2048]{1,0:T(8,128)(2,1)S(1)} %copy-done.11, bf16[2048,2304]{1,0:T(8,128)(2,1)} %refs_11_.1, bf16[256,2304]{1,0:T(8,128)(2,1)S(1)} %copy-done.2, bf16[256,2048]{1,0:T(8,128)(2,1)S(1)} %copy-done.9, ...), custom_call_target="tpu_custom_call" | custom-call | flops 2415919104 | bytes 18874368 | tf_op jit(solution)/shard_map/pallas_call | solution.py:158
  600.3 4.8 all-gather.14.cloned.1.call-done.refs_2_.refs_9_
  611.2 27.9 %shard_map.98 = (bf16[256,2048]{1,0:T(8,128)(2,1)S(1)}, bf16[256,2048]{1,0:T(8,128)(2,1)}, bf16[256,2048]{1,0:T(8,128)(2,1)S(1)}) custom-call(bf16[256,2048]{1,0:T(8,128)(2,1)S(1)} %copy-done.14, bf16[2048,2304]{1,0:T(8,128)(2,1)} %refs_11_.1, bf16[256,2304]{1,0:T(8,128)(2,1)S(1)} %copy-done.4, bf16[256,2048]{1,0:T(8,128)(2,1)S(1)} %copy-done.12, ...), custom_call_target="tpu_custom_call" | custom-call | flops 2415919104 | bytes 18874368 | tf_op jit(solution)/shard_map/pallas_call | solution.py:158
  655.3 18.9 %shard_map.100 = f32[2048,2304]{1,0:T(8,128)} custom-call(bf16[256,2048]{1,0:T(8,128)(2,1)S(1)} %copy-done.59, bf16[256,2048]{1,0:T(8,128)(2,1)S(1)} %copy-done.62, bf16[256,2048]{1,0:T(8,128)(2,1)S(1)} %copy-done.65, bf16[256,2048]{1,0:T(8,128)(2,1)S(1)} %copy-done.68, bf16[256,2048]{1,0:T(8,128)(2,1)S(1)} %copy-done.71, bf16[256,2304]{1,0:T(8,128)(2,1)S(1)} %copy-done.33, ...), custom_call_target="tpu_custom_call" | custom-call | flops 12079595520 | bytes 28311552 | tf_op jit(solution)/shard_map/pallas_call | solution.py:205
  677.3 17.5 %shard_map.102 = (f32[2304,2048]{1,0:T(8,128)}, f32[1,2048]{1,0:T(1,128)}) custom-call(bf16[1280,2304]{1,0:T(8,128)(2,1)} %refs_0_.1, bf16[256,2048]{1,0:T(8,128)(2,1)S(1)} %copy-done.75, bf16[256,2048]{1,0:T(8,128)(2,1)S(1)} %copy-done.77, bf16[256,2048]{1,0:T(8,128)(2,1)S(1)} %copy-done.79, bf16[256,2048]{1,0:T(8,128)(2,1)S(1)} %copy-done.52, ...), custom_call_target="tpu_custom_call" | custom-call | flops 12079595520 | bytes 18874368 | tf_op jit(solution)/shard_map/pallas_call | solution.py:247
  (208 shorter events, 99.0 us)
Async XLA Ops:
  7.2 133.2 %reduce-scatter.6.cloned.1.call-start = ((), (), s32[]{:S(2)}) async-start(), calls=%async_computation.5 | async-start | bytes 2506752 | tf_op jit(solution)/shard_map/reduce_scatter | solution.py:334
  17.6 27.9 %copy-start.73 = (f32[2048]{0:T(1024)S(1)}, f32[2048]{0:T(1024)}, u32[]{:S(2)}) copy-start(f32[2048]{0:T(1024)} %param.7) | copy-start | bytes 24580
  45.5 27.2 %copy-start.25 = (bf16[256,2048]{1,0:T(8,128)(2,1)}, bf16[256,2048]{1,0:T(8,128)(2,1)S(1)}, u32[]{:S(2)}) copy-start(bf16[256,2048]{1,0:T(8,128)(2,1)S(1)} %get-tuple-element.64.refs_5_.refs_6_) | copy-start | bytes 3145732
  76.1 131.1 %reduce-scatter.8.cloned.1.call-start = ((), (), s32[]{:S(2)}) async-start(), calls=%async_computation.7 | async-start | bytes 2506752 | tf_op jit(solution)/shard_map/reduce_scatter | solution.py:334
  108.9 138.0 %all-gather.6.cloned.1.call-start = ((), (), s32[]{:S(2)}) async-start(), calls=%async_computation.6 | async-start | bytes 1253376 | tf_op jit(solution)/shard_map/all_gather | solution.py:309
  142.0 171.0 %reduce-scatter.10.cloned.1.call-start = ((), (), s32[]{:S(2)}) async-start(), calls=%async_computation.9 | async-start | bytes 2506752 | tf_op jit(solution)/shard_map/reduce_scatter | solution.py:334
  176.0 176.8 %all-gather.8.cloned.1.call-start = ((), (), s32[]{:S(2)}) async-start(), calls=%async_computation.8 | async-start | bytes 1253376 | tf_op jit(solution)/shard_map/all_gather | solution.py:309
  208.8 210.6 %reduce-scatter.12.cloned.1.call-start = ((), (), s32[]{:S(2)}) async-start(), calls=%async_computation.11 | async-start | bytes 2506752 | tf_op jit(solution)/shard_map/reduce_scatter | solution.py:334
  283.3 175.8 %all-gather.10.cloned.1.call-start = ((), (), s32[]{:S(2)}) async-start(), calls=%async_computation.10 | async-start | bytes 1253376 | tf_op jit(solution)/shard_map/all_gather | solution.py:309
  314.7 210.7 %reduce-scatter.14.cloned.1.call-start = ((), (), s32[]{:S(2)}) async-start(), calls=%async_computation.13 | async-start | bytes 2506752 | tf_op jit(solution)/shard_map/reduce_scatter | solution.py:334
  389.2 176.1 %all-gather.12.cloned.1.call-start = ((), (), s32[]{:S(2)}) async-start(), calls=%async_computation.12 | async-start | bytes 1253376 | tf_op jit(solution)/shard_map/all_gather | solution.py:309
  421.1 184.0 %all-gather.14.cloned.1.call-start = ((), (), s32[]{:S(2)}) async-start(), calls=%async_computation.14 | async-start | bytes 1253376 | tf_op jit(solution)/shard_map/all_gather | solution.py:309
  421.3 7.3 %copy-start.58 = (bf16[256,2048]{1,0:T(8,128)(2,1)S(1)}, bf16[256,2048]{1,0:T(8,128)(2,1)}, u32[]{:S(2)}) copy-start(bf16[256,2048]{1,0:T(8,128)(2,1)} %copy-done.57) | copy-start | bytes 3145732
  421.3 7.5 %copy-start.61 = (bf16[256,2048]{1,0:T(8,128)(2,1)S(1)}, bf16[256,2048]{1,0:T(8,128)(2,1)}, u32[]{:S(2)}) copy-start(bf16[256,2048]{1,0:T(8,128)(2,1)} %copy-done.60) | copy-start | bytes 3145732
  427.1 3.7 collective-permute-start
  495.3 70.1 %copy-start.17 = (bf16[256,2048]{1,0:T(8,128)(2,1)S(1)}, bf16[256,2048]{1,0:T(8,128)(2,1)}, u32[]{:S(2)}) copy-start(bf16[256,2048]{1,0:T(8,128)(2,1)} %copy-done.15) | copy-start | bytes 3145732
  611.2 27.9 %copy-start.21 = (bf16[256,2048]{1,0:T(8,128)(2,1)S(1)}, bf16[256,2048]{1,0:T(8,128)(2,1)}, u32[]{:S(2)}) copy-start(bf16[256,2048]{1,0:T(8,128)(2,1)} %copy-done.18) | copy-start | bytes 3145732
  611.2 27.9 %copy-start.42 = (bf16[256,2048]{1,0:T(8,128)(2,1)S(1)}, bf16[256,2048]{1,0:T(8,128)(2,1)}, u32[]{:S(2)}) copy-start(bf16[256,2048]{1,0:T(8,128)(2,1)} %copy-done.40) | copy-start | bytes 3145732
  641.4 4.4 copy-start.3
  641.4 5.2 copy-start.35
  641.4 32.8 %collective-permute-start.1 = (bf16[256,2048]{1,0:T(8,128)(2,1)}, bf16[256,2048]{1,0:T(8,128)(2,1)}, u32[]{:S(2)}, u32[]{:S(2)}) collective-permute-start(bf16[256,2048]{1,0:T(8,128)(2,1)} %get-tuple-element.107.refs_0_), channel_id=1, source_target_pairs={{0,16},{16,0},{1,17},{17,1},{2,18},{18,2},{3,19},{19,3},{4,20},{20... | collective-permute-start | bytes 3145736 | tf_op jit(solution)/shard_map/ppermute | solution.py:272
  655.3 18.9 %copy-start.39 = (bf16[256,2048]{1,0:T(8,128)(2,1)S(1)}, bf16[256,2048]{1,0:T(8,128)(2,1)}, u32[]{:S(2)}) copy-start(bf16[256,2048]{1,0:T(8,128)(2,1)} %copy-done.36) | copy-start | bytes 3145732
  655.3 18.9 %copy-start.45 = (bf16[256,2048]{1,0:T(8,128)(2,1)S(1)}, bf16[256,2048]{1,0:T(8,128)(2,1)}, u32[]{:S(2)}) copy-start(bf16[256,2048]{1,0:T(8,128)(2,1)} %copy-done.43) | copy-start | bytes 3145732
  674.2 3.1 copy-start.79
  (69 other events, 88.5 us)
Sparse Core Ops, SparseCore 0:
  76.2 64.1 reduce-scatter.5
  145.2 62.0 reduce-scatter.7
  209.5 37.3 all-gather.5
  251.1 61.9 reduce-scatter.9
  315.4 37.3 all-gather.7
  357.5 61.9 reduce-scatter.11
  421.7 37.3 all-gather.9
  463.4 61.8 reduce-scatter.13
  527.9 37.3 all-gather.11
  567.7 37.3 all-gather.13
